TPU v7x, 32 devices: a whole 2x2x4 slice. The times are simulated.
32 devices in a mesh: fsdp: 8 (over y, x, core), dp: 4 (over z).
Axes of the slice: x: 2, y: 2, z: 4, core: 2. Of those that a mesh axis runs over, the one named last changes fastest.
Arguments:
- teacher_hidden: bfloat16 [256, 8192], P(('fsdp', 'dp'))
- student_hidden: bfloat16 [256, 4096], P(('fsdp', 'dp'))
- teacher_head: bfloat16 [8192, 16384], P('dp', 'fsdp'), may hold values from -0.1875 to 0.1875
- student_head: bfloat16 [4096, 16384], P('dp', 'fsdp'), may hold values from -0.25 to 0.25
- actions: int32 [256], replicated, may hold values from 0 to 16383
- advantages: float32 [256], replicated, may hold values from -0.21875 to 0.21875
- loss_mask: int32 [256], replicated, may hold values 0 or 1
Outputs:
- token_loss: float32 [256], P('dp')
- head_grad: float32 [4096, 16384], P('dp', 'fsdp')
- hidden_grad: bfloat16 [256, 4096], P('fsdp', 'dp')
All inputs are finite; a program needn't handle non-finite values.
Results may differ from a plain program's by a relative error of at most 0.0048.
Values may be sent and summed in bfloat16 or wider, within the bound.
A program may use at most 128 MiB of HBM per device.

v0:
```python
import jax
import jax.numpy as jnp
from jax import lax
from jax.sharding import PartitionSpec as P

kl_weight = 0.5


def shards(
    teacher_hidden, student_hidden, teacher_head, student_head, actions, advantages, loss_mask
):
    teacher_part, student_part = (
        lax.all_to_all(teacher_hidden, "dp", split_axis=1, concat_axis=0, tiled=True),
        lax.all_to_all(student_hidden, "dp", split_axis=1, concat_axis=0, tiled=True),
    )
    teacher_rows, student_rows = (
        lax.all_gather(teacher_part, "fsdp", axis=0, tiled=True),
        lax.all_gather(student_part, "fsdp", axis=0, tiled=True),
    )
    total_rows = teacher_rows.shape[0]
    share = total_rows // lax.axis_size("dp")
    teacher_partial = jnp.dot(teacher_rows, teacher_head, preferred_element_type=jnp.float32)
    student_partial = jnp.dot(student_rows, student_head, preferred_element_type=jnp.float32)
    teacher_logits, student_logits = (
        lax.psum_scatter(teacher_partial, "dp", scatter_dimension=0, tiled=True),
        lax.psum_scatter(student_partial, "dp", scatter_dimension=0, tiled=True),
    )
    first_row = lax.axis_index("dp") * share
    chosen = lax.dynamic_slice_in_dim(actions, first_row, share)
    benefit = lax.dynamic_slice_in_dim(advantages, first_row, share)
    weight = lax.dynamic_slice_in_dim(loss_mask, first_row, share).astype(jnp.float32)
    vocab_shard = teacher_logits.shape[1]
    columns = lax.axis_index("fsdp") * vocab_shard + jnp.arange(vocab_shard, dtype=jnp.int32)
    onehot = (chosen[:, None] == columns[None, :]).astype(jnp.float32)
    local_pick = jnp.sum(onehot * student_logits, axis=1)
    teacher_max, student_max = lax.pmax(
        (jnp.max(teacher_logits, axis=1), jnp.max(student_logits, axis=1)), "fsdp"
    )
    teacher_exp = jnp.exp(teacher_logits - teacher_max[:, None])
    student_exp = jnp.exp(student_logits - student_max[:, None])
    teacher_sum, student_sum, cross, pick = lax.psum(
        (
            jnp.sum(teacher_exp, axis=1),
            jnp.sum(student_exp, axis=1),
            jnp.sum(teacher_exp * (teacher_logits - student_logits), axis=1),
            local_pick,
        ),
        "fsdp",
    )
    teacher_lse = teacher_max + jnp.log(teacher_sum)
    student_lse = student_max + jnp.log(student_sum)
    kl = cross / teacher_sum - teacher_lse + student_lse
    action_logp = pick - student_lse
    losses = weight * (kl_weight * kl - benefit * action_logp)
    teacher_prob = teacher_exp / teacher_sum[:, None]
    student_prob = student_exp / student_sum[:, None]
    logit_grad = (
        weight[:, None]
        * (kl_weight * (student_prob - teacher_prob) + benefit[:, None] * (student_prob - onehot))
    ).astype(jnp.bfloat16)
    grad_all = lax.all_gather(logit_grad, "dp", axis=0, tiled=True)
    head_grad = lax.dot_general(
        student_rows, grad_all, (((0,), (0,)), ((), ())), preferred_element_type=jnp.float32
    )
    hidden_grad = lax.psum_scatter(
        lax.dot_general(
            grad_all, student_head, (((1,), (1,)), ((), ())), preferred_element_type=jnp.float32
        ),
        "fsdp",
        scatter_dimension=0,
        tiled=True,
    ).astype(jnp.bfloat16)
    return (losses, head_grad, hidden_grad)


def solution(mesh):
    placed = (
        P(("fsdp", "dp"), None),
        P(("fsdp", "dp"), None),
        P("dp", "fsdp"),
        P("dp", "fsdp"),
        P(),
        P(),
        P(),
    )
    return jax.shard_map(
        shards,
        mesh=mesh,
        in_specs=placed,
        out_specs=(P("dp"), P("dp", "fsdp"), P("fsdp", "dp")),
        check_vma=False,
    )
```

profile of v0, /device:TPU:0, one launch (start us, length us, event | category | flops | bytes accessed | tf_op | source)
XLA Modules:
  0.0 238.3 jit_solution(6707249504238443248)
XLA Ops:
  8.0 0.0 all-gather.3.cloned.1.call-start
  8.0 12.5 %all_to_all.38 = bf16[8,4,2048]{2,0,1:T(8,128)(2,1)} all-to-all(bf16[8,4,2048]{2,0,1:T(8,128)(2,1)} %bitcast.20), channel_id=1, replica_groups=mesh['fsdp'=8,'dp'=4] {'dp'}, dimensions={1} | all-to-all | bytes 262144 | tf_op jit(solution)/shard_map/all_to_all | solution.py:13
  20.6 0.0 all-gather.3.cloned.1.call-update
  20.6 0.0 reduce-scatter.6.cloned.1.call-start
  20.6 9.0 %all_to_all.39 = bf16[8,4,1024]{2,0,1:T(8,128)(2,1)S(1)} all-to-all(bf16[8,4,1024]{2,0,1:T(8,128)(2,1)} %bitcast.21), channel_id=1, replica_groups=mesh['fsdp'=8,'dp'=4] {'dp'}, dimensions={1} | all-to-all | bytes 131072 | tf_op jit(solution)/shard_map/all_to_all | solution.py:14
  29.6 9.8 %all_gather.10 = bf16[256,1024]{1,0:T(8,128)(2,1)S(1)} all-gather(bf16[32,1024]{1,0:T(8,128)(2,1)S(1)} %bitcast.19), channel_id=1, replica_groups=mesh['fsdp'=8,'dp'=4] {'fsdp'}, dimensions={0}, use_global_device_ids=true | all-gather | bytes 589824 | tf_op jit(solution)/shard_map/all_gather | solution.py:18
  39.5 4.8 %fusion.9 = f32[256,2048]{1,0:T(8,128)} fusion(bf16[256,1024]{1,0:T(8,128)(2,1)S(1)} %all_gather.10, bf16[1024,2048]{1,0:T(8,128)(2,1)} %param.10), kind=kOutput, calls=%fused_computation.18 | convolution fusion | flops 1073741824 | bytes 6815744 | tf_op jit(solution)/shard_map/dot_general | solution.py:23
  44.3 0.0 reduce-scatter.6.cloned.1.call-update
  44.3 0.0 reduce-scatter.4.cloned.1.call-start
  44.4 0.0 all-gather.3.cloned.1.call-done
  44.4 7.4 %fusion.8 = f32[256,2048]{1,0:T(8,128)} fusion(bf16[256,2048]{1,0:T(8,128)(2,1)} %all-gather.3.cloned.1.call-done, bf16[2048,2048]{1,0:T(8,128)(2,1)} %param.9), kind=kOutput, calls=%fused_computation.17 | convolution fusion | flops 2147483648 | bytes 11534336 | tf_op jit(solution)/shard_map/dot_general | solution.py:22
  51.8 0.0 reduce-scatter.4.cloned.1.call-update
  51.8 0.0 all-gather.5.cloned.1.call-start
  51.9 0.1 dynamic_slice.11
  52.0 34.5 %reduce-scatter.6.cloned.1.call-done = f32[64,2048]{1,0:T(8,128)} async-done(((f32[256,2048]{1,0:T(8,128)}), f32[64,2048]{1,0:T(8,128)}) %reduce-scatter.6.cloned.1.call-update) | async-done | bytes 524304 | tf_op jit(solution)/shard_map/reduce_scatter | solution.py:26
  86.5 1.2 reduce_max.19
  87.6 44.4 %reduce-scatter.4.cloned.1.call-done = f32[64,2048]{1,0:T(8,128)} async-done(((f32[256,2048]{1,0:T(8,128)}), f32[64,2048]{1,0:T(8,128)}) %reduce-scatter.4.cloned.1.call-update) | async-done | bytes 524304 | tf_op jit(solution)/shard_map/reduce_scatter | solution.py:25
  132.0 1.2 reduce_max.18
  133.2 13.2 %all-reduce.1 = (f32[64]{0:T(128)S(1)}, f32[64]{0:T(128)S(1)}) all-reduce(f32[64]{0:T(128)S(1)} %reduce_max.18, f32[64]{0:T(128)S(1)} %reduce_max.19), channel_id=1, replica_groups=mesh['fsdp'=8,'dp'=4] {'fsdp'}, use_global_device_ids=true, to_apply=%region_2.0 | all-reduce | flops 128 | bytes 1024 | tf_op jit(solution)/shard_map/pmax | solution.py:36
  146.5 1.6 multiply_reduce_fusion
  148.1 11.8 %all-reduce = (f32[64]{0:T(128)S(1)}, f32[64]{0:T(128)S(1)}, f32[64]{0:T(128)S(1)}, f32[64]{0:T(128)S(1)}) all-reduce(f32[64]{0:T(128)S(1)} %get-tuple-element.8, f32[64]{0:T(128)S(1)} %get-tuple-element.9, f32[64]{0:T(128)S(1)} %get-tuple-element.7, f32[64]{0:T(128)S(1)} %get-tuple-element.6), channel_id=1, replica_groups=mesh['fsdp'=8,'dp'=4] {'fsdp'}, use_global_device_ids=true, to_apply=%region_13.0 | all-reduce | flops 256 | bytes 2048 | tf_op jit(solution)/shard_map/psum | solution.py:41
  159.9 0.6 subtract_multiply_fusion
  160.5 2.3 fusion.5
  162.8 0.0 all-gather.5.cloned.1.call-update
  162.8 0.0 reduce-scatter.8.cloned.1.call-start
  162.9 25.7 %all-gather.5.cloned.1.call-done = bf16[256,2048]{1,0:T(8,128)(2,1)} async-done(((bf16[64,2048]{1,0:T(8,128)(2,1)}), bf16[256,2048]{1,0:T(8,128)(2,1)}) %all-gather.5.cloned.1.call-update) | async-done | bytes 1048592 | tf_op jit(solution)/shard_map/all_gather | solution.py:61
  188.6 4.9 %fusion.10 = f32[256,1024]{1,0:T(8,128)} fusion(bf16[256,2048]{1,0:T(8,128)(2,1)} %all-gather.5.cloned.1.call-done, bf16[1024,2048]{1,0:T(8,128)(2,1)} %param.10), kind=kOutput, calls=%fused_computation.19 | convolution fusion | flops 1073741824 | bytes 6291456 | tf_op jit(solution)/shard_map/dot_general | solution.py:66
  193.5 0.0 reduce-scatter.8.cloned.1.call-update
  193.6 4.5 %convolution_bitcast_fusion = f32[1024,2048]{0,1:T(8,128)} fusion(bf16[256,2048]{1,0:T(8,128)(2,1)S(1)} %copy-done, bf16[256,1024]{1,0:T(8,128)(2,1)S(1)} %all_gather.10), kind=kOutput, calls=%fused_computation | convolution fusion | flops 1073741824 | bytes 9961472 | tf_op jit(solution)/shard_map/dot_general | solution.py:62
  198.1 9.2 %copy.10 = f32[1024,2048]{1,0:T(8,128)} copy(f32[1024,2048]{0,1:T(8,128)} %convolution_bitcast_fusion) | data formatting | bytes 16777216
  207.3 21.9 %reduce-scatter.8.cloned.1.call-done = f32[32,1024]{1,0:T(8,128)} async-done(((f32[256,1024]{1,0:T(8,128)}), f32[32,1024]{1,0:T(8,128)}) %reduce-scatter.8.cloned.1.call-update) | async-done | bytes 131088 | tf_op jit(solution)/shard_map/reduce_scatter | solution.py:65
  229.1 1.5 convert_element_type.15
  (9 shorter events, 0.0 us)
Async XLA Ops:
  8.0 36.4 %all-gather.3.cloned.1.call-start = ((), (), s32[]{:S(2)}) async-start(), calls=%async_computation.5 | async-start | bytes 1179648 | tf_op jit(solution)/shard_map/all_gather | solution.py:17
  20.6 65.9 %reduce-scatter.6.cloned.1.call-start = ((), (), s32[]{:S(2)}) async-start(), calls=%async_computation.7 | async-start | bytes 2621440 | tf_op jit(solution)/shard_map/reduce_scatter | solution.py:26
  44.3 7.6 %copy-start.3 = (s32[256]{0:T(256)S(1)}, s32[256]{0:T(256)}, u32[]{:S(2)}) copy-start(s32[256]{0:T(256)} %param.11) | copy-start | bytes 3076
  44.3 87.7 %reduce-scatter.4.cloned.1.call-start = ((), (), s32[]{:S(2)}) async-start(), calls=%async_computation.6 | async-start | bytes 2621440 | tf_op jit(solution)/shard_map/reduce_scatter | solution.py:25
  51.8 108.1 %copy-start.1 = (f32[256]{0:T(256)S(1)}, f32[256]{0:T(256)}, u32[]{:S(2)}) copy-start(f32[256]{0:T(256)} %param.12) | copy-start | bytes 3076
  51.8 108.1 %copy-start.2 = (s32[256]{0:T(256)S(1)}, s32[256]{0:T(256)}, u32[]{:S(2)}) copy-start(s32[256]{0:T(256)} %param.13) | copy-start | bytes 3076
  51.8 136.8 %all-gather.5.cloned.1.call-start = ((), (), s32[]{:S(2)}) async-start(), calls=%async_computation.8 | async-start | bytes 1310720 | tf_op jit(solution)/shard_map/all_gather | solution.py:61
  162.8 66.3 %reduce-scatter.8.cloned.1.call-start = ((), (), s32[]{:S(2)}) async-start(), calls=%async_computation.9 | async-start | bytes 1179648 | tf_op jit(solution)/shard_map/reduce_scatter | solution.py:65
  188.6 5.0 %copy-start = (bf16[256,2048]{1,0:T(8,128)(2,1)S(1)}, bf16[256,2048]{1,0:T(8,128)(2,1)}, u32[]{:S(2)}) copy-start(bf16[256,2048]{1,0:T(8,128)(2,1)} %all-gather.5.cloned.1.call-done) | copy-start | bytes 3145732
Sparse Core Ops, SparseCore 0:
  20.7 22.7 all-gather.2
  193.7 35.4 reduce-scatter.7
Sparse Core Ops, SparseCore 1:
  44.4 42.0 reduce-scatter.5
  89.3 42.7 reduce-scatter.3
  162.9 25.6 all-gather.4
where the time goes:
time: 239 us; the launch traced here: 238 us
  waiting for transfers between devices  127 us (53%)
  blocking collectives  56.4 us (24%)
  matrix products  21.6 us (9%)
  between operations  15.7 us (7%)
  local copies, waits for them, and re-layouts  9.29 us (4%)
  other arithmetic  8.42 us (4%)
    reduce_scatter x1, waiting for transfers between devices, shards(): lax.psum_scatter(teacher_partial, 'dp', scatter_dimension=0, tiled=True)  44.4 us
    reduce_scatter x1, waiting for transfers between devices, shards(): lax.psum_scatter(student_partial, 'dp', scatter_dimension=0, tiled=True)  34.5 us
    all_gather x1, waiting for transfers between devices, shards(): grad_all = lax.all_gather(logit_grad, 'dp', axis=0, tiled=True)  25.7 us
    reduce_scatter x1, waiting for transfers between devices, shards(): lax.psum_scatter(lax.dot_general(grad_all, student_head, (((1,), (1,)), (...  21.9 us
    pmax x1, blocking collectives, shards(): lax.pmax((jnp.max(teacher_logits, axis=1), jnp.max(student_logits, axis=1...  13.2 us
    all_to_all x1, blocking collectives, shards(): lax.all_to_all(teacher_hidden, 'dp', split_axis=1, concat_axis=0, tiled=T...  12.5 us
    psum x1, blocking collectives, shards(): lax.psum((jnp.sum(teacher_exp, axis=1), jnp.sum(student_exp, axis=1), jnp...  11.8 us
    all_gather x1, blocking collectives, shards(): lax.all_gather(student_part, 'fsdp', axis=0, tiled=True)  9.85 us
  transfers between devices with their start and end apart: 5, of which 4 were waited for; matrix products, arithmetic and copies ran while one was open for 11% of the time, Pallas kernels for 0%

commit v1 on v0

v1 whole, which is shorter than its diff:
```python
import functools

import jax
import jax.numpy as jnp
from jax import lax
from jax.experimental import pallas as pl
from jax.experimental.pallas import tpu as pltpu
from jax.sharding import PartitionSpec as P

KL_WEIGHT = 0.5
MESH = pl.DeviceIdType.MESH
PIECE = 32
LANES = 128
STEPS = 128.0
FULL = 32000.0
f32, bf16, i32, i16 = jnp.float32, jnp.bfloat16, jnp.int32, jnp.int16


def encode(x, out_ref):
    cols = x.shape[1]
    top = jnp.maximum(jnp.max(jnp.abs(x), axis=1, keepdims=True), 1e-30)
    code = jnp.floor(jnp.log2(top) * STEPS) + 2.0
    q = jnp.floor(x * (jnp.exp2(code * (-1.0 / STEPS)) * FULL) + 0.5)
    out_ref[:, :cols] = q.astype(i32).astype(i16)
    out_ref[:, cols:] = jnp.broadcast_to(code, (x.shape[0], LANES)).astype(i32).astype(i16)


def decode(in_ref, cols):
    code = in_ref[:, cols:].astype(i32).astype(f32)[:, 0:1]
    scale = jnp.exp2(code * (1.0 / STEPS)) * (1.0 / FULL)
    return in_ref[:, :cols].astype(i32).astype(f32) * scale


def main_kernel(
    F, D,
    th_ref, sh_ref, wt_hbm, ws_hbm, act_ref, adv_ref, mask_ref,
    loss_ref, hid_ref, rows_out, grad_out,
    wt, ws, zt, zs, gt, gs, rows_t, rows_s, part_t, part_s, line, xcol, stats, ycol, acol, lossbuf, grads, hg, pair_in, peer_in,
    w_sem, z_send, z_recv, ag_send, ag_recv, pr_send, pr_recv, l_send, l_recv, st_send, st_recv, g_send, g_recv,
    hp_send, hp_recv, hd_send, hd_recv, ls_send, ls_recv, out_sem,
):
    f, r = lax.axis_index("fsdp"), lax.axis_index("dp")
    T, V = part_t.shape
    J, H = F // 2, T // 2
    core, j = lax.rem(f, 2), f // 2
    partner = f + 1 - 2 * core
    upper = (r >= D // 2).astype(i32)
    step = 1 - 2 * upper
    end = jnp.minimum(r, D - 1 - r) == 0
    nblk = H // LANES
    NG = H // PIECE
    TB = T // F

    def remote(src, dst, ssem, rsem, **dev):
        return pltpu.make_async_remote_copy(
            src_ref=src, dst_ref=dst, send_sem=ssem, recv_sem=rsem, device_id=dev, device_id_type=MESH)

    w_s = pltpu.make_async_copy(ws_hbm, ws, w_sem.at[0])
    w_t = pltpu.make_async_copy(wt_hbm, wt, w_sem.at[1])
    w_s.start()
    w_t.start()

    barrier = pltpu.get_barrier_semaphore()
    for k in range(1, F):
        pl.semaphore_signal(barrier, inc=1, device_id={"fsdp": lax.rem(f + k, F)}, device_id_type=MESH)
    for k in range(1, D):
        pl.semaphore_signal(barrier, inc=1, device_id={"dp": lax.rem(r + k, D)}, device_id_type=MESH)

    hidden = ((sh_ref, zs, gs), (th_ref, zt, gt))
    for src, z, _ in hidden:
        x = src[...].astype(f32)
        half = z.shape[-1]
        for d in range(D):
            lo = x[:, 2 * d * half:(2 * d + 1) * half]
            hi = x[:, (2 * d + 1) * half:(2 * d + 2) * half]
            z[d] = jnp.concatenate([lo, hi], axis=0).astype(bf16)
    pl.semaphore_wait(barrier, F - 1 + D - 1)

    def z_copy(m, k):
        to = lax.rem(r + k, D)
        return remote(hidden[m][1].at[to], hidden[m][2].at[f, r], z_send.at[m, k], z_recv.at[m, k], dp=to)

    def z_in(m, k):
        return remote(hidden[m][1].at[0], hidden[m][2].at[f, lax.rem(r + D - k, D)], z_send.at[m, k], z_recv.at[m, k], dp=r)

    for m in range(2):
        for k in range(1, D):
            z_copy(m, k).start()
        hidden[m][2][f, r] = hidden[m][1][r]

    own = upper * H
    for b in range(nblk):
        a = act_ref[:, pl.ds(pl.multiple_of(own + b * LANES, LANES), LANES)].astype(f32)
        acol[b * LANES:(b + 1) * LANES, :] = jnp.broadcast_to(a, (LANES, LANES)).T

    def ag_copy(m, k):
        g = hidden[m][2]
        return remote(g.at[f], g.at[f], ag_send.at[m, k], ag_recv.at[m, k], fsdp=lax.rem(j + k, J) * 2 + core)

    def ag_slot(k):
        return lax.rem(j + J - k, J) * 2

    def pr_copy(m, k):
        g = hidden[m][2]
        s = ag_slot(k) + core
        return remote(g.at[s], g.at[s], pr_send.at[m, k], pr_recv.at[m, k], fsdp=partner)

    def pr_in(m, k):
        g = hidden[m][2]
        s = ag_slot(k) + 1 - core
        return remote(g.at[s], g.at[s], pr_send.at[m, k], pr_recv.at[m, k], fsdp=partner)

    for m in range(2):
        for k in range(1, D):
            z_in(m, k).wait_recv()
        for k in range(1, J):
            ag_copy(m, k).start()
        pr_copy(m, 0).start()

    def gather(m, rows):
        g = hidden[m][2]
        for k in range(1, J):
            s = ag_slot(k) + core
            remote(g.at[s], g.at[s], ag_send.at[m, k], ag_recv.at[m, k], fsdp=partner).wait_recv()
            pr_copy(m, k).start()
        for k in range(J):
            pr_in(m, k).wait_recv()
        half = g.shape[-1]
        n = g.shape[1] * 8

        @pl.loop(0, F)
        def _(b):
            x = g[b].astype(f32)
            at = pl.ds(pl.multiple_of(b * n, n), n)
            rows[at, :half] = x[:, 0:8, :].reshape(n, half).astype(bf16)
            rows[at, half:] = x[:, 8:16, :].reshape(n, half).astype(bf16)

    tile = min(512, V)

    def project(rows, w, part):
        @pl.loop(0, V // tile)
        def _(c):
            at = pl.ds(pl.multiple_of(c * tile, tile), tile)
            part[:, at] = jnp.dot(rows[...], w[:, at], preferred_element_type=f32)

    def line_copy(flow, i):
        to = jnp.clip(r + 1 - 2 * flow, 0, D - 1)
        return remote(line.at[flow, i], line.at[flow, i], l_send.at[flow, i], l_recv.at[flow, i], dp=to)

    near, far = upper, 1 - upper
    parts = (part_s, part_t)

    def own_rows(flow, i):
        return pl.ds(pl.multiple_of((1 - flow) * H + i * PIECE, PIECE), PIECE)

    def begin(m):
        @pl.when(end)
        def _():
            @pl.loop(0, NG)
            def _(i):
                encode(parts[m][own_rows(near, i), :], line.at[near, m * NG + i])
                line_copy(near, m * NG + i).start()

    def relay(m):
        @pl.when(jnp.logical_not(end))
        def _():
            @pl.loop(0, NG)
            def _(i):
                for flow in (near, far):
                    line_copy(flow, m * NG + i).wait_recv()
                    x = parts[m][own_rows(flow, i), :] + decode(line.at[flow, m * NG + i], V)
                    encode(x, line.at[flow, m * NG + i])
                    line_copy(flow, m * NG + i).start()

    def finish(m):
        @pl.loop(0, NG)
        def _(i):
            line_copy(far, m * NG + i).wait_recv()
            at = own_rows(far, i)
            parts[m][at, :] = parts[m][at, :] + decode(line.at[far, m * NG + i], V)

    gather(0, rows_s)
    w_s.wait()
    project(rows_s, ws, part_s)
    begin(0)
    rows_save = pltpu.make_async_copy(rows_s, rows_out, out_sem.at[0])
    rows_save.start()
    gather(1, rows_t)
    w_t.wait()
    project(rows_t, wt, part_t)
    begin(1)
    relay(0)
    relay(1)

    def st_copy(k):
        return remote(stats.at[f], stats.at[f], st_send.at[k], st_recv.at[k], fsdp=lax.rem(f + k, F))

    def st_in(k):
        s = lax.rem(f + F - k, F)
        return remote(stats.at[s], stats.at[s], st_send.at[k], st_recv.at[k], fsdp=s)

    def g_copy(half, i):
        at = pl.ds(pl.multiple_of(half * H + i * PIECE, PIECE), PIECE)
        to = jnp.clip(r + 1 - 2 * half, 0, D - 1)
        return remote(grads.at[at], grads.at[at], g_send.at[half, i], g_recv.at[half, i], dp=to)

    def loss_copy(k):
        return remote(lossbuf, lossbuf, ls_send.at[k], ls_recv.at[0], dp=r + step * k)

    lane = lax.broadcasted_iota(i32, (PIECE, LANES), 1)
    column = lax.broadcasted_iota(i32, (PIECE, V), 1) + f * V

    @pl.when(end)
    def _():
        finish(0)
        finish(1)

        @pl.loop(0, NG)
        def _(i):
            at = own_rows(far, i)
            here = pl.ds(pl.multiple_of(i * PIECE, PIECE), PIECE)
            lt, ls = part_t[at, :], part_s[at, :]
            mt, ms = jnp.max(lt, axis=1, keepdims=True), jnp.max(ls, axis=1, keepdims=True)
            et = jnp.exp(lt - mt)
            hit = column == acol[here, 0:1].astype(i32)
            values = (
                mt, ms, jnp.sum(et, axis=1, keepdims=True), jnp.sum(jnp.exp(ls - ms), axis=1, keepdims=True),
                jnp.sum(et * (lt - ls), axis=1, keepdims=True),
                jnp.sum(jnp.where(hit, ls, 0.0), axis=1, keepdims=True))
            x = jnp.zeros((PIECE, LANES), f32)
            for n, v in enumerate(values):
                x = jnp.where(lane == n, v, x)
            xcol[here, :] = x

        for b in range(nblk):
            stats[f, b * 8:(b + 1) * 8, :] = xcol[b * LANES:(b + 1) * LANES, :].T[0:8, :]
        for k in range(1, F):
            st_copy(k).start()
        for k in range(1, F):
            st_in(k).wait_recv()
        for b in range(nblk):
            s = stats[:, b * 8:(b + 1) * 8, :]
            mt, ms = s[:, 0:1, :], s[:, 1:2, :]
            top_t, top_s = jnp.max(mt, axis=0), jnp.max(ms, axis=0)
            scale_t = jnp.exp(mt - top_t[None])
            sum_t = jnp.sum(s[:, 2:3, :] * scale_t, axis=0)
            sum_s = jnp.sum(s[:, 3:4, :] * jnp.exp(ms - top_s[None]), axis=0)
            cross = jnp.sum(s[:, 4:5, :] * scale_t, axis=0)
            pick = jnp.sum(s[:, 5:6, :], axis=0)
            lse_t, lse_s = top_t + jnp.log(sum_t), top_s + jnp.log(sum_s)
            at = pl.ds(pl.multiple_of(own + b * LANES, LANES), LANES)
            weight, benefit = mask_ref[:, at].astype(f32), adv_ref[:, at]
            kl = cross / sum_t - lse_t + lse_s
            loss = weight * (KL_WEIGHT * kl - benefit * (pick - lse_s))
            lossbuf[b * 8:(b + 1) * 8, :] = jnp.broadcast_to(loss, (8, LANES))
            y = jnp.concatenate(
                [jnp.broadcast_to(v, (8, LANES)) for v in (lse_t, lse_s, weight, benefit)]
                + [jnp.zeros((LANES - 32, LANES), f32)], axis=0)
            ycol[b * LANES:(b + 1) * LANES, :] = y.T

        @pl.loop(0, NG)
        def _(i):
            at = own_rows(far, i)
            here = pl.ds(pl.multiple_of(i * PIECE, PIECE), PIECE)
            lse_t, lse_s = ycol[here, 0:1], ycol[here, 8:9]
            weight, benefit = ycol[here, 16:17], ycol[here, 24:25]
            tp, sp = jnp.exp(part_t[at, :] - lse_t), jnp.exp(part_s[at, :] - lse_s)
            hit = (column == acol[here, 0:1].astype(i32)).astype(f32)
            g = weight * (KL_WEIGHT * (sp - tp) + benefit * (sp - hit))
            grads[at, :] = g.astype(bf16)
            g_copy(upper, i).start()

        for k in range(1, D // 2):
            loss_copy(k).start()

    feature = ws.shape[0]
    ftile = min(256, feature)

    def back(half):
        at = pl.ds(pl.multiple_of(half * H, H), H)

        @pl.loop(0, feature // ftile)
        def _(c):
            cols = pl.ds(pl.multiple_of(c * ftile, ftile), ftile)
            y = lax.dot_general(grads[at, :], ws[cols, :], (((1,), (1,)), ((), ())), preferred_element_type=f32)
            hg[pl.ds(half * (J // 2), J // 2), :, :, cols] = y.reshape(J // 2, 2, TB, ftile)

    @pl.when(jnp.logical_not(end))
    def _():
        @pl.loop(0, NG)
        def _(i):
            g_copy(upper, i).wait_recv()
            g_copy(upper, i).start()
            g_copy(1 - upper, i).wait_recv()
            g_copy(1 - upper, i).start()
        back(upper)

    @pl.when(end)
    def _():
        back(upper)

        @pl.loop(0, NG)
        def _(i):
            g_copy(1 - upper, i).wait_recv()

    grad_save = pltpu.make_async_copy(grads, grad_out, out_sem.at[1])
    grad_save.start()
    back(1 - upper)

    pair = remote(hg.at[:, 1 - core], pair_in, hp_send, hp_recv, fsdp=partner)
    pair.start()
    pair.wait()

    @pl.loop(0, J)
    def _(b):
        hg[b, core] = hg[b, core] + pair_in[b]

    def hd_copy(k):
        to = lax.rem(j + k, J)
        return remote(hg.at[to, core], peer_in.at[j], hd_send.at[k], hd_recv.at[k], fsdp=to * 2 + core)

    def hd_in(k):
        s = lax.rem(j + J - k, J)
        return remote(hg.at[0, core], peer_in.at[s], hd_send.at[k], hd_recv.at[k], fsdp=f)

    for k in range(1, J):
        hd_copy(k).start()
    peer_in[j] = hg[j, core]

    @pl.when(jnp.logical_not(end))
    def _():
        loss_copy(0).wait_recv()
    for b in range(nblk):
        loss_ref[:, b * LANES:(b + 1) * LANES] = lossbuf[b * 8:b * 8 + 1, :]

    for k in range(1, J):
        hd_in(k).wait_recv()
    hid_ref[...] = jnp.sum(peer_in[...], axis=0).astype(bf16)

    for m in range(2):
        for k in range(1, D):
            z_copy(m, k).wait_send()
        for k in range(1, J):
            ag_copy(m, k).wait_send()
        for k in range(J):
            pr_copy(m, k).wait_send()
    for k in range(1, J):
        hd_copy(k).wait_send()

    @pl.loop(0, 2 * NG)
    def _(i):
        line_copy(near, i).wait_send()

    @pl.loop(0, NG)
    def _(i):
        g_copy(upper, i).wait_send()

    @pl.when(end)
    def _():
        for k in range(1, F):
            st_copy(k).wait_send()
        for k in range(1, D // 2):
            loss_copy(k).wait_send()

    @pl.when(jnp.logical_not(end))
    def _():
        @pl.loop(0, 2 * NG)
        def _(i):
            line_copy(far, i).wait_send()

        @pl.loop(0, NG)
        def _(i):
            g_copy(1 - upper, i).wait_send()

    rows_save.wait()
    grad_save.wait()


def head_grad_kernel(rows_ref, grad_ref, out_ref):
    out_ref[...] = lax.dot_general(
        rows_ref[...], grad_ref[...], (((0,), (0,)), ((), ())), preferred_element_type=f32)


def shards(F, D, teacher_hidden, student_hidden, teacher_head, student_head, actions, advantages, loss_mask):
    T = actions.shape[0]
    kt, V = teacher_head.shape
    ks = student_head.shape[0]
    mine = teacher_hidden.shape[0]
    J, H, TB = F // 2, T // 2, T // F
    NG, nblk = H // PIECE, H // LANES
    vmem = pl.BlockSpec(memory_space=pltpu.VMEM)
    hbm = pl.BlockSpec(memory_space=pl.ANY)
    dma = pltpu.SemaphoreType.DMA
    loss, hidden_grad, rows, grads = pl.pallas_call(
        functools.partial(main_kernel, F, D),
        out_shape=(
            jax.ShapeDtypeStruct((1, H), f32),
            jax.ShapeDtypeStruct((TB, ks), bf16),
            jax.ShapeDtypeStruct((T, ks), bf16),
            jax.ShapeDtypeStruct((T, V), bf16),
        ),
        in_specs=[vmem, vmem, hbm, hbm, vmem, vmem, vmem],
        out_specs=(vmem, vmem, hbm, hbm),
        scratch_shapes=[
            pltpu.VMEM((kt, V), bf16),
            pltpu.VMEM((ks, V), bf16),
            pltpu.VMEM((D, 2 * mine, kt // 2), bf16),
            pltpu.VMEM((D, 2 * mine, ks // 2), bf16),
            pltpu.VMEM((F, D, 2 * mine, kt // 2), bf16),
            pltpu.VMEM((F, D, 2 * mine, ks // 2), bf16),
            pltpu.VMEM((T, kt), bf16),
            pltpu.VMEM((T, ks), bf16),
            pltpu.VMEM((T, V), f32),
            pltpu.VMEM((T, V), f32),
            pltpu.VMEM((2, 2 * NG, PIECE, V + LANES), i16),
            pltpu.VMEM((H, LANES), f32),
            pltpu.VMEM((F, nblk * 8, LANES), f32),
            pltpu.VMEM((H, LANES), f32),
            pltpu.VMEM((H, LANES), f32),
            pltpu.VMEM((nblk * 8, LANES), f32),
            pltpu.VMEM((T, V), bf16),
            pltpu.VMEM((J, 2, TB, ks), f32),
            pltpu.VMEM((J, TB, ks), f32),
            pltpu.VMEM((J, TB, ks), f32),
            dma((2,)),
            dma((2, D)), dma((2, D)),
            dma((2, J)), dma((2, J)),
            dma((2, J)), dma((2, J)),
            dma((2, 2 * NG)), dma((2, 2 * NG)),
            dma((F,)), dma((F,)),
            dma((2, NG)), dma((2, NG)),
            dma, dma,
            dma((J,)), dma((J,)),
            dma((D,)), dma((1,)),
            dma((2,)),
        ],
        compiler_params=pltpu.CompilerParams(
            collective_id=0, has_side_effects=True, vmem_limit_bytes=63 * 2**20),
    )(teacher_hidden, student_hidden, teacher_head, student_head,
      actions.reshape(1, T), advantages.reshape(1, T), loss_mask.reshape(1, T))
    tile = min(256, V)
    head_grad = pl.pallas_call(
        head_grad_kernel,
        grid=(V // tile,),
        out_shape=jax.ShapeDtypeStruct((ks, V), f32),
        in_specs=[pl.BlockSpec((T, ks), lambda c: (0, 0)), pl.BlockSpec((T, tile), lambda c: (0, c))],
        out_specs=pl.BlockSpec((ks, tile), lambda c: (0, c)),
        compiler_params=pltpu.CompilerParams(vmem_limit_bytes=32 * 2**20),
    )(rows, grads)
    share = T // D
    first = lax.rem(lax.axis_index("dp"), D // 2) * share
    losses = lax.dynamic_slice_in_dim(loss.reshape(H), first, share)
    return losses, head_grad, hidden_grad


def solution(mesh):
    placed = (
        P(("fsdp", "dp"), None),
        P(("fsdp", "dp"), None),
        P("dp", "fsdp"),
        P("dp", "fsdp"),
        P(),
        P(),
        P(),
    )
    return jax.shard_map(
        functools.partial(shards, mesh.shape["fsdp"], mesh.shape["dp"]),
        mesh=mesh,
        in_specs=placed,
        out_specs=(P("dp"), P("dp", "fsdp"), P("fsdp", "dp")),
        check_vma=False,
    )
```

time: 239 us -> 125 us (0.52)
  waiting for transfers between devices: 127 us -> 0 us
  Pallas kernels: 0 us -> 120 us
  blocking collectives: 56.4 us -> 0 us
  matrix products: 21.6 us -> 0 us
  between operations: 15.7 us -> 0.65 us
  other arithmetic: 8.42 us -> 0 us
  local copies, waits for them, and re-layouts: 9.29 us -> 4.11 us
    pallas_call x0 -> x2, Pallas kernels: none -> 120 us  [the longest x1 114 us: shards(): pl.pallas_call(functools.partial(main_kernel, F, D), out_shape=(jax.Shape...]
    reduce_scatter x3 -> x0, waiting for transfers between devices: 101 us -> none  [the longest x1 44.4 us: shards(): lax.psum_scatter(teacher_partial, 'dp', scatter_dimension=0, tiled=True)]
    all_gather x2 -> x0, waiting for transfers between devices: 25.7 us -> none  [the longest x1 25.7 us: shards(): grad_all = lax.all_gather(logit_grad, 'dp', axis=0, tiled=True)]
    dot_general x4 -> x0, matrix products: 21.6 us -> none  [the longest x1 7.37 us: shards(): jnp.dot(teacher_rows, teacher_head, preferred_element_type=jnp.float32)]
    all_to_all x2 -> x0, blocking collectives: 21.5 us -> none  [the longest x1 12.5 us: shards(): lax.all_to_all(teacher_hidden, 'dp', split_axis=1, concat_axis=0, tiled=T...]
    pmax x1 -> x0, blocking collectives: 13.2 us -> none  [shards(): lax.pmax((jnp.max(teacher_logits, axis=1), jnp.max(student_logits, axis=1...]
    psum x1 -> x0, blocking collectives: 11.8 us -> none  [shards(): lax.psum((jnp.sum(teacher_exp, axis=1), jnp.sum(student_exp, axis=1), jnp...]
    all_gather x1 -> x0, blocking collectives: 9.85 us -> none  [shards(): lax.all_gather(student_part, 'fsdp', axis=0, tiled=True)]
  transfers between devices with their start and end apart: 5 -> 0, of which waited for: 4 -> 0; matrix products, arithmetic and copies ran while one was open for 11% -> 0% of each run, Pallas kernels for 0% -> 0%
where the time goes in v1:
time: 125 us
  Pallas kernels  120 us (96%)
  local copies, waits for them, and re-layouts  4.11 us (3%)
    pallas_call x1, Pallas kernels, shards(): pl.pallas_call(functools.partial(main_kernel, F, D), out_shape=(jax.Shape...  114 us
    pallas_call x1, Pallas kernels, shards(): pl.pallas_call(head_grad_kernel, grid=(V // tile,), out_shape=jax.ShapeDt...  5.79 us
    unnamed x7, local copies, waits for them, and re-layouts  2.9 us

profile of v1, /device:TPU:0, one launch (start us, length us, event | category | flops | bytes accessed | tf_op | source)
XLA Modules:
  0.0 125.0 jit_solution(6537478711038577378)
XLA Ops:
  0.6 114.5 %shard_map.94 = (f32[1,128]{1,0:T(1,128)}, bf16[32,1024]{1,0:T(8,128)(2,1)}, bf16[256,1024]{1,0:T(8,128)(2,1)}, bf16[256,2048]{1,0:T(8,128)(2,1)}) custom-call(bf16[8,8192]{1,0:T(8,128)(2,1)} %th_ref.1, bf16[8,4096]{1,0:T(8,128)(2,1)} %sh_ref.1, bf16[2048,2048]{1,0:T(8,128)(2,1)} %wt_hbm.1, bf16[1024,2048]{1,0:T(8,128)(2,1)} %ws_hbm.1, s32[1,256]{1,0:T(1,128)} %bitcast.5, ...), custom_call_target="tpu_custom_call" | custom-call | tf_op jit(solution)/shard_map/pallas_call | solution.py:394
  115.1 1.2 dynamic-slice_bitcast_fusion
  116.3 0.0 copy-start
  116.3 1.2 copy-done
  117.6 0.0 copy-start.1
  117.6 1.0 copy-done.1
  118.6 0.0 copy-start.2
  118.6 5.8 %shard_map.95 = f32[1024,2048]{1,0:T(8,128)} custom-call(bf16[256,1024]{1,0:T(8,128)(2,1)S(1)} %copy-done.1, bf16[256,2048]{1,0:T(8,128)(2,1)S(1)} %copy-done), custom_call_target="tpu_custom_call" | custom-call | tf_op jit(solution)/shard_map/pallas_call | solution.py:442
  124.4 0.0 copy-done.2
  124.4 0.6 copy.11
Async XLA Ops:
  116.3 1.2 copy-start
  117.6 1.0 copy-start.1
  118.6 5.8 %copy-start.2 = (bf16[32,1024]{1,0:T(8,128)(2,1)S(1)}, bf16[32,1024]{1,0:T(8,128)(2,1)}, u32[]{:S(2)}) copy-start(bf16[32,1024]{1,0:T(8,128)(2,1)} %get-tuple-element.16) | copy-start | bytes 196612

commit v2 on v1

--- a/solution.py
+++ b/solution.py
@@ -10,6 +10,9 @@
 KL_WEIGHT = 0.5
 MESH = pl.DeviceIdType.MESH
 PIECE = 32
+GPIECE = 16
+LAG = 2
+GLAG = 3
 LANES = 128
 STEPS = 128.0
 FULL = 32000.0
@@ -35,12 +38,12 @@
     F, D,
     th_ref, sh_ref, wt_hbm, ws_hbm, act_ref, adv_ref, mask_ref,
     loss_ref, hid_ref, rows_out, grad_out,
-    wt, ws, zt, zs, gt, gs, rows_t, rows_s, part_t, part_s, line, xcol, stats, ycol, acol, lossbuf, grads, hg, pair_in, peer_in,
+    wt, ws, zt, zs, gt, gs, rows_t, rows_s, part, line, xcol, stats, ycol, acol, lossbuf, grads, hg, pair_in, peer_in,
     w_sem, z_send, z_recv, ag_send, ag_recv, pr_send, pr_recv, l_send, l_recv, st_send, st_recv, g_send, g_recv,
     hp_send, hp_recv, hd_send, hd_recv, ls_send, ls_recv, out_sem,
 ):
     f, r = lax.axis_index("fsdp"), lax.axis_index("dp")
-    T, V = part_t.shape
+    _, T, V = part.shape
     J, H = F // 2, T // 2
     core, j = lax.rem(f, 2), f // 2
     partner = f + 1 - 2 * core
@@ -49,6 +52,7 @@
     end = jnp.minimum(r, D - 1 - r) == 0
     nblk = H // LANES
     NG = H // PIECE
+    GG = H // GPIECE
     TB = T // F
 
     def remote(src, dst, ssem, rsem, **dev):
@@ -137,18 +141,17 @@
 
     tile = min(512, V)
 
-    def project(rows, w, part):
+    def project(rows, w, m):
         @pl.loop(0, V // tile)
         def _(c):
             at = pl.ds(pl.multiple_of(c * tile, tile), tile)
-            part[:, at] = jnp.dot(rows[...], w[:, at], preferred_element_type=f32)
+            part[m, :, at] = jnp.dot(rows[...], w[:, at], preferred_element_type=f32)
 
     def line_copy(flow, i):
         to = jnp.clip(r + 1 - 2 * flow, 0, D - 1)
         return remote(line.at[flow, i], line.at[flow, i], l_send.at[flow, i], l_recv.at[flow, i], dp=to)
 
     near, far = upper, 1 - upper
-    parts = (part_s, part_t)
 
     def own_rows(flow, i):
         return pl.ds(pl.multiple_of((1 - flow) * H + i * PIECE, PIECE), PIECE)
@@ -158,39 +161,47 @@
         def _():
             @pl.loop(0, NG)
             def _(i):
-                encode(parts[m][own_rows(near, i), :], line.at[near, m * NG + i])
+                encode(part[m, own_rows(near, i), :], line.at[near, m * NG + i])
                 line_copy(near, m * NG + i).start()
 
-    def relay(m):
+    def pass_on(flow, p):
+        line_copy(flow, p).wait_recv()
+        x = part[p // NG, own_rows(flow, lax.rem(p, NG)), :] + decode(line.at[flow, p], V)
+        encode(x, line.at[flow, p])
+        line_copy(flow, p).start()
+
+    def relay(first, last):
         @pl.when(jnp.logical_not(end))
         def _():
-            @pl.loop(0, NG)
-            def _(i):
-                for flow in (near, far):
-                    line_copy(flow, m * NG + i).wait_recv()
-                    x = parts[m][own_rows(flow, i), :] + decode(line.at[flow, m * NG + i], V)
-                    encode(x, line.at[flow, m * NG + i])
-                    line_copy(flow, m * NG + i).start()
-
-    def finish(m):
-        @pl.loop(0, NG)
-        def _(i):
-            line_copy(far, m * NG + i).wait_recv()
-            at = own_rows(far, i)
-            parts[m][at, :] = parts[m][at, :] + decode(line.at[far, m * NG + i], V)
+            @pl.loop(first, last)
+            def _(p):
+                @pl.when(p < 2 * NG)
+                def _():
+                    pass_on(near, p)
+
+                @pl.when(p >= LAG)
+                def _():
+                    pass_on(far, p - LAG)
+
+    def finish(m, i):
+        line_copy(far, m * NG + i).wait_recv()
+        at = own_rows(far, i)
+        x = part[m, at, :] + decode(line.at[far, m * NG + i], V)
+        part[m, at, :] = x
+        return x
 
     gather(0, rows_s)
     w_s.wait()
-    project(rows_s, ws, part_s)
+    project(rows_s, ws, 0)
     begin(0)
     rows_save = pltpu.make_async_copy(rows_s, rows_out, out_sem.at[0])
     rows_save.start()
     gather(1, rows_t)
+    relay(0, NG // 2)
     w_t.wait()
-    project(rows_t, wt, part_t)
+    project(rows_t, wt, 1)
     begin(1)
-    relay(0)
-    relay(1)
+    relay(NG // 2, 2 * NG + LAG)
 
     def st_copy(k):
         return remote(stats.at[f], stats.at[f], st_send.at[k], st_recv.at[k], fsdp=lax.rem(f + k, F))
@@ -200,7 +211,7 @@
         return remote(stats.at[s], stats.at[s], st_send.at[k], st_recv.at[k], fsdp=s)
 
     def g_copy(half, i):
-        at = pl.ds(pl.multiple_of(half * H + i * PIECE, PIECE), PIECE)
+        at = pl.ds(pl.multiple_of(half * H + i * GPIECE, GPIECE), GPIECE)
         to = jnp.clip(r + 1 - 2 * half, 0, D - 1)
         return remote(grads.at[at], grads.at[at], g_send.at[half, i], g_recv.at[half, i], dp=to)
 
@@ -212,14 +223,15 @@
 
     @pl.when(end)
     def _():
-        finish(0)
-        finish(1)
-
         @pl.loop(0, NG)
         def _(i):
-            at = own_rows(far, i)
+            finish(0, i)
+
+        @pl.loop(0, NG)
+        def _(i):
             here = pl.ds(pl.multiple_of(i * PIECE, PIECE), PIECE)
-            lt, ls = part_t[at, :], part_s[at, :]
+            lt = finish(1, i)
+            ls = part[0, own_rows(far, i), :]
             mt, ms = jnp.max(lt, axis=1, keepdims=True), jnp.max(ls, axis=1, keepdims=True)
             et = jnp.exp(lt - mt)
             hit = column == acol[here, 0:1].astype(i32)
@@ -264,11 +276,12 @@
             here = pl.ds(pl.multiple_of(i * PIECE, PIECE), PIECE)
             lse_t, lse_s = ycol[here, 0:1], ycol[here, 8:9]
             weight, benefit = ycol[here, 16:17], ycol[here, 24:25]
-            tp, sp = jnp.exp(part_t[at, :] - lse_t), jnp.exp(part_s[at, :] - lse_s)
+            tp, sp = jnp.exp(part[1, at, :] - lse_t), jnp.exp(part[0, at, :] - lse_s)
             hit = (column == acol[here, 0:1].astype(i32)).astype(f32)
             g = weight * (KL_WEIGHT * (sp - tp) + benefit * (sp - hit))
             grads[at, :] = g.astype(bf16)
-            g_copy(upper, i).start()
+            for n in range(PIECE // GPIECE):
+                g_copy(upper, i * (PIECE // GPIECE) + n).start()
 
         for k in range(1, D // 2):
             loss_copy(k).start()
@@ -285,56 +298,78 @@
             y = lax.dot_general(grads[at, :], ws[cols, :], (((1,), (1,)), ((), ())), preferred_element_type=f32)
             hg[pl.ds(half * (J // 2), J // 2), :, :, cols] = y.reshape(J // 2, 2, TB, ftile)
 
+    def pair_copy(b):
+        return remote(hg.at[b, 1 - core], pair_in.at[b], hp_send.at[b], hp_recv.at[b], fsdp=partner)
+
+    def hd_copy(b):
+        return remote(hg.at[b, core], peer_in.at[j], hd_send.at[b], hd_recv.at[j], fsdp=b * 2 + core)
+
+    def hd_in(b):
+        return remote(hg.at[b, core], peer_in.at[b], hd_send.at[b], hd_recv.at[b], fsdp=f)
+
+    def pair_start(half):
+        @pl.loop(0, J // 2)
+        def _(n):
+            pair_copy(half * (J // 2) + n).start()
+
+    def share_out(half):
+        @pl.loop(0, J // 2)
+        def _(n):
+            b = half * (J // 2) + n
+            pair_copy(b).wait()
+            y = hg[b, core] + pair_in[b]
+
+            @pl.when(b == j)
+            def _():
+                peer_in[j] = y
+
+            @pl.when(b != j)
+            def _():
+                hg[b, core] = y
+                hd_copy(b).start()
+
     @pl.when(jnp.logical_not(end))
     def _():
-        @pl.loop(0, NG)
-        def _(i):
-            g_copy(upper, i).wait_recv()
-            g_copy(upper, i).start()
-            g_copy(1 - upper, i).wait_recv()
-            g_copy(1 - upper, i).start()
-        back(upper)
+        @pl.loop(0, GG + GLAG)
+        def _(i):
+            @pl.when(i < GG)
+            def _():
+                g_copy(upper, i).wait_recv()
+                g_copy(upper, i).start()
+
+            @pl.when(i >= GLAG)
+            def _():
+                g_copy(1 - upper, i - GLAG).wait_recv()
+                g_copy(1 - upper, i - GLAG).start()
+
+    back(upper)
+    pair_start(upper)
+    share_out(upper)
 
     @pl.when(end)
     def _():
-        back(upper)
-
-        @pl.loop(0, NG)
+        @pl.loop(0, GG)
         def _(i):
             g_copy(1 - upper, i).wait_recv()
 
     grad_save = pltpu.make_async_copy(grads, grad_out, out_sem.at[1])
     grad_save.start()
     back(1 - upper)
-
-    pair = remote(hg.at[:, 1 - core], pair_in, hp_send, hp_recv, fsdp=partner)
-    pair.start()
-    pair.wait()
-
-    @pl.loop(0, J)
-    def _(b):
-        hg[b, core] = hg[b, core] + pair_in[b]
-
-    def hd_copy(k):
-        to = lax.rem(j + k, J)
-        return remote(hg.at[to, core], peer_in.at[j], hd_send.at[k], hd_recv.at[k], fsdp=to * 2 + core)
-
-    def hd_in(k):
-        s = lax.rem(j + J - k, J)
-        return remote(hg.at[0, core], peer_in.at[s], hd_send.at[k], hd_recv.at[k], fsdp=f)
-
-    for k in range(1, J):
-        hd_copy(k).start()
-    peer_in[j] = hg[j, core]
+    pair_start(1 - upper)
+    share_out(1 - upper)
 
     @pl.when(jnp.logical_not(end))
     def _():
         loss_copy(0).wait_recv()
-    for b in range(nblk):
-        loss_ref[:, b * LANES:(b + 1) * LANES] = lossbuf[b * 8:b * 8 + 1, :]
+    losses = jnp.concatenate([lossbuf[b * 8:b * 8 + 1, :] for b in range(nblk)], axis=1)
+    share = T // D
+    for q in range(D // 2):
+        @pl.when(lax.rem(r, D // 2) == q)
+        def _():
+            loss_ref[...] = losses[:, q * share:(q + 1) * share]
 
     for k in range(1, J):
-        hd_in(k).wait_recv()
+        hd_in(lax.rem(j + k, J)).wait_recv()
     hid_ref[...] = jnp.sum(peer_in[...], axis=0).astype(bf16)
 
     for m in range(2):
@@ -345,13 +380,13 @@
         for k in range(J):
             pr_copy(m, k).wait_send()
     for k in range(1, J):
-        hd_copy(k).wait_send()
+        hd_copy(lax.rem(j + k, J)).wait_send()
 
     @pl.loop(0, 2 * NG)
     def _(i):
         line_copy(near, i).wait_send()
 
-    @pl.loop(0, NG)
+    @pl.loop(0, GG)
     def _(i):
         g_copy(upper, i).wait_send()
 
@@ -368,7 +403,7 @@
         def _(i):
             line_copy(far, i).wait_send()
 
-        @pl.loop(0, NG)
+        @pl.loop(0, GG)
         def _(i):
             g_copy(1 - upper, i).wait_send()
 
@@ -387,14 +422,14 @@
     ks = student_head.shape[0]
     mine = teacher_hidden.shape[0]
     J, H, TB = F // 2, T // 2, T // F
-    NG, nblk = H // PIECE, H // LANES
+    NG, GG, nblk = H // PIECE, H // GPIECE, H // LANES
     vmem = pl.BlockSpec(memory_space=pltpu.VMEM)
     hbm = pl.BlockSpec(memory_space=pl.ANY)
     dma = pltpu.SemaphoreType.DMA
     loss, hidden_grad, rows, grads = pl.pallas_call(
         functools.partial(main_kernel, F, D),
         out_shape=(
-            jax.ShapeDtypeStruct((1, H), f32),
+            jax.ShapeDtypeStruct((1, T // D), f32),
             jax.ShapeDtypeStruct((TB, ks), bf16),
             jax.ShapeDtypeStruct((T, ks), bf16),
             jax.ShapeDtypeStruct((T, V), bf16),
@@ -410,8 +445,7 @@
             pltpu.VMEM((F, D, 2 * mine, ks // 2), bf16),
             pltpu.VMEM((T, kt), bf16),
             pltpu.VMEM((T, ks), bf16),
-            pltpu.VMEM((T, V), f32),
-            pltpu.VMEM((T, V), f32),
+            pltpu.VMEM((2, T, V), f32),
             pltpu.VMEM((2, 2 * NG, PIECE, V + LANES), i16),
             pltpu.VMEM((H, LANES), f32),
             pltpu.VMEM((F, nblk * 8, LANES), f32),
@@ -428,8 +462,8 @@
             dma((2, J)), dma((2, J)),
             dma((2, 2 * NG)), dma((2, 2 * NG)),
             dma((F,)), dma((F,)),
-            dma((2, NG)), dma((2, NG)),
-            dma, dma,
+            dma((2, GG)), dma((2, GG)),
+            dma((J,)), dma((J,)),
             dma((J,)), dma((J,)),
             dma((D,)), dma((1,)),
             dma((2,)),
@@ -445,12 +479,9 @@
         out_shape=jax.ShapeDtypeStruct((ks, V), f32),
         in_specs=[pl.BlockSpec((T, ks), lambda c: (0, 0)), pl.BlockSpec((T, tile), lambda c: (0, c))],
         out_specs=pl.BlockSpec((ks, tile), lambda c: (0, c)),
-        compiler_params=pltpu.CompilerParams(vmem_limit_bytes=32 * 2**20),
+        compiler_params=pltpu.CompilerParams(vmem_limit_bytes=63 * 2**20),
     )(rows, grads)
-    share = T // D
-    first = lax.rem(lax.axis_index("dp"), D // 2) * share
-    losses = lax.dynamic_slice_in_dim(loss.reshape(H), first, share)
-    return losses, head_grad, hidden_grad
+    return loss.reshape(T // D), head_grad, hidden_grad
 
 
 def solution(mesh):

time: 125 us -> 103 us (0.82)
  Pallas kernels: 120 us -> 100 us
  local copies, waits for them, and re-layouts: 4.11 us -> 1.15 us
    pallas_call x1, Pallas kernels: 114 us -> 92.7 us  [shards(): pl.pallas_call(functools.partial(main_kernel, F, D), out_shape=(jax.Shape...]
    pallas_call x1, Pallas kernels: 5.79 us -> 7.78 us  [shards(): pl.pallas_call(head_grad_kernel, grid=(V // tile,), out_shape=jax.ShapeDt...]
    unnamed x7 -> x6, local copies, waits for them, and re-layouts: 2.9 us -> 1.15 us
where the time goes in v2:
time: 103 us; the launch traced here: 102 us
  Pallas kernels  100 us (97%)
  local copies, waits for them, and re-layouts  1.15 us (1%)
    pallas_call x1, Pallas kernels, shards(): pl.pallas_call(functools.partial(main_kernel, F, D), out_shape=(jax.Shape...  92.7 us
    pallas_call x1, Pallas kernels, shards(): pl.pallas_call(head_grad_kernel, grid=(V // tile,), out_shape=jax.ShapeDt...  7.78 us

profile of v2, /device:TPU:0, one launch (start us, length us, event | category | flops | bytes accessed | tf_op | source)
XLA Modules:
  0.0 102.2 jit_solution(6668310088566146289)
XLA Ops:
  0.6 92.7 %shard_map.94 = (f32[1,64]{1,0:T(1,128)}, bf16[32,1024]{1,0:T(8,128)(2,1)}, bf16[256,1024]{1,0:T(8,128)(2,1)}, bf16[256,2048]{1,0:T(8,128)(2,1)}) custom-call(bf16[8,8192]{1,0:T(8,128)(2,1)} %th_ref.1, bf16[8,4096]{1,0:T(8,128)(2,1)} %sh_ref.1, bf16[2048,2048]{1,0:T(8,128)(2,1)} %wt_hbm.1, bf16[1024,2048]{1,0:T(8,128)(2,1)} %ws_hbm.1, s32[1,256]{1,0:T(1,128)} %bitcast.4, ...), custom_call_target="tpu_custom_call" | custom-call | tf_op jit(solution)/shard_map/pallas_call | solution.py:429
  93.3 0.0 copy-start.1
  93.3 0.0 copy-start
  93.3 7.8 %shard_map.95 = f32[1024,2048]{1,0:T(8,128)} custom-call(bf16[256,1024]{1,0:T(8,128)(2,1)} %get-tuple-element.8.rows_ref, bf16[256,2048]{1,0:T(8,128)(2,1)} %get-tuple-element.9.grad_ref), custom_call_target="tpu_custom_call" | custom-call | tf_op jit(solution)/shard_map/pallas_call | solution.py:476
  101.1 0.0 copy-done.1
  101.1 0.5 copy.12
  101.6 0.0 copy-done
  101.6 0.6 copy.13
Async XLA Ops:
  93.3 7.8 %copy-start.1 = (f32[1,64]{1,0:T(1,128)S(1)}, f32[1,64]{1,0:T(1,128)}, u32[]{:S(2)}) copy-start(f32[1,64]{1,0:T(1,128)} %get-tuple-element.7) | copy-start | bytes 772
  93.3 8.3 %copy-start = (bf16[32,1024]{1,0:T(8,128)(2,1)S(1)}, bf16[32,1024]{1,0:T(8,128)(2,1)}, u32[]{:S(2)}) copy-start(bf16[32,1024]{1,0:T(8,128)(2,1)} %get-tuple-element.16) | copy-start | bytes 196612

commit v3 on v2

--- a/solution.py
+++ b/solution.py
@@ -13,6 +13,7 @@
 GPIECE = 16
 LAG = 2
 GLAG = 3
+CHUNK = 64
 LANES = 128
 STEPS = 128.0
 FULL = 32000.0
@@ -38,7 +39,7 @@
     F, D,
     th_ref, sh_ref, wt_hbm, ws_hbm, act_ref, adv_ref, mask_ref,
     loss_ref, hid_ref, rows_out, grad_out,
-    wt, ws, zt, zs, gt, gs, rows_t, rows_s, part, line, xcol, stats, ycol, acol, lossbuf, grads, hg, pair_in, peer_in,
+    wt, ws, zt, zs, gt, gs, rows_t, rows_s, part, line, xcol, stats, ycol, acol, lossbuf, grads, pair_in, peer_in,
     w_sem, z_send, z_recv, ag_send, ag_recv, pr_send, pr_recv, l_send, l_recv, st_send, st_recv, g_send, g_recv,
     hp_send, hp_recv, hd_send, hd_recv, ls_send, ls_recv, out_sem,
 ):
@@ -50,7 +51,7 @@
     upper = (r >= D // 2).astype(i32)
     step = 1 - 2 * upper
     end = jnp.minimum(r, D - 1 - r) == 0
-    nblk = H // LANES
+    nblk, NC = H // LANES, H // CHUNK
     NG = H // PIECE
     GG = H // GPIECE
     TB = T // F
@@ -139,7 +140,7 @@
             rows[at, :half] = x[:, 0:8, :].reshape(n, half).astype(bf16)
             rows[at, half:] = x[:, 8:16, :].reshape(n, half).astype(bf16)
 
-    tile = min(512, V)
+    tile = max(LANES, min(V, 2**17 // T))
 
     def project(rows, w, m):
         @pl.loop(0, V // tile)
@@ -194,8 +195,6 @@
     w_s.wait()
     project(rows_s, ws, 0)
     begin(0)
-    rows_save = pltpu.make_async_copy(rows_s, rows_out, out_sem.at[0])
-    rows_save.start()
     gather(1, rows_t)
     relay(0, NG // 2)
     w_t.wait()
@@ -203,12 +202,22 @@
     begin(1)
     relay(NG // 2, 2 * NG + LAG)
 
-    def st_copy(k):
-        return remote(stats.at[f], stats.at[f], st_send.at[k], st_recv.at[k], fsdp=lax.rem(f + k, F))
-
-    def st_in(k):
+    rows_x = wt.at[:ws.shape[0], :T]
+
+    @pl.loop(0, T // LANES)
+    def _(b):
+        at = pl.ds(pl.multiple_of(b * LANES, LANES), LANES)
+        rows_x[:, at] = rows_s[at, :].astype(f32).T.astype(bf16)
+
+    rows_save = pltpu.make_async_copy(rows_x, rows_out, out_sem.at[0])
+    rows_save.start()
+
+    def st_copy(c, k):
+        return remote(stats.at[c, f], stats.at[c, f], st_send.at[c, k], st_recv.at[c, k], fsdp=lax.rem(f + k, F))
+
+    def st_in(c, k):
         s = lax.rem(f + F - k, F)
-        return remote(stats.at[s], stats.at[s], st_send.at[k], st_recv.at[k], fsdp=s)
+        return remote(stats.at[c, s], stats.at[c, s], st_send.at[c, k], st_recv.at[c, k], fsdp=s)
 
     def g_copy(half, i):
         at = pl.ds(pl.multiple_of(half * H + i * GPIECE, GPIECE), GPIECE)
@@ -223,35 +232,39 @@
 
     @pl.when(end)
     def _():
+        xcol[...] = jnp.zeros_like(xcol)
+
         @pl.loop(0, NG)
         def _(i):
             finish(0, i)
 
-        @pl.loop(0, NG)
-        def _(i):
-            here = pl.ds(pl.multiple_of(i * PIECE, PIECE), PIECE)
-            lt = finish(1, i)
-            ls = part[0, own_rows(far, i), :]
-            mt, ms = jnp.max(lt, axis=1, keepdims=True), jnp.max(ls, axis=1, keepdims=True)
-            et = jnp.exp(lt - mt)
-            hit = column == acol[here, 0:1].astype(i32)
-            values = (
-                mt, ms, jnp.sum(et, axis=1, keepdims=True), jnp.sum(jnp.exp(ls - ms), axis=1, keepdims=True),
-                jnp.sum(et * (lt - ls), axis=1, keepdims=True),
-                jnp.sum(jnp.where(hit, ls, 0.0), axis=1, keepdims=True))
-            x = jnp.zeros((PIECE, LANES), f32)
-            for n, v in enumerate(values):
-                x = jnp.where(lane == n, v, x)
-            xcol[here, :] = x
-
-        for b in range(nblk):
-            stats[f, b * 8:(b + 1) * 8, :] = xcol[b * LANES:(b + 1) * LANES, :].T[0:8, :]
-        for k in range(1, F):
-            st_copy(k).start()
-        for k in range(1, F):
-            st_in(k).wait_recv()
-        for b in range(nblk):
-            s = stats[:, b * 8:(b + 1) * 8, :]
+        def finish_chunk(c):
+            block = pl.ds(c * CHUNK // LANES * LANES, LANES)
+            first, last = c * CHUNK // PIECE, (c + 1) * CHUNK // PIECE
+
+            @pl.loop(first, last)
+            def _(i):
+                here = pl.ds(pl.multiple_of(i * PIECE, PIECE), PIECE)
+                lt = finish(1, i)
+                ls = part[0, own_rows(far, i), :]
+                mt, ms = jnp.max(lt, axis=1, keepdims=True), jnp.max(ls, axis=1, keepdims=True)
+                et = jnp.exp(lt - mt)
+                hit = column == acol[here, 0:1].astype(i32)
+                values = (
+                    mt, ms, jnp.sum(et, axis=1, keepdims=True), jnp.sum(jnp.exp(ls - ms), axis=1, keepdims=True),
+                    jnp.sum(et * (lt - ls), axis=1, keepdims=True),
+                    jnp.sum(jnp.where(hit, ls, 0.0), axis=1, keepdims=True))
+                x = jnp.zeros((PIECE, LANES), f32)
+                for n, v in enumerate(values):
+                    x = jnp.where(lane == n, v, x)
+                xcol[here, :] = x
+
+            stats[c, f] = xcol[block, :].T[0:8, :]
+            for k in range(1, F):
+                st_copy(c, k).start()
+            for k in range(1, F):
+                st_in(c, k).wait_recv()
+            s = stats[c]
             mt, ms = s[:, 0:1, :], s[:, 1:2, :]
             top_t, top_s = jnp.max(mt, axis=0), jnp.max(ms, axis=0)
             scale_t = jnp.exp(mt - top_t[None])
@@ -260,28 +273,32 @@
             cross = jnp.sum(s[:, 4:5, :] * scale_t, axis=0)
             pick = jnp.sum(s[:, 5:6, :], axis=0)
             lse_t, lse_s = top_t + jnp.log(sum_t), top_s + jnp.log(sum_s)
-            at = pl.ds(pl.multiple_of(own + b * LANES, LANES), LANES)
+            at = pl.ds(pl.multiple_of(own + c * CHUNK // LANES * LANES, LANES), LANES)
             weight, benefit = mask_ref[:, at].astype(f32), adv_ref[:, at]
             kl = cross / sum_t - lse_t + lse_s
             loss = weight * (KL_WEIGHT * kl - benefit * (pick - lse_s))
-            lossbuf[b * 8:(b + 1) * 8, :] = jnp.broadcast_to(loss, (8, LANES))
+            lossbuf[c * 8:(c + 1) * 8, :] = jnp.broadcast_to(loss, (8, LANES))
             y = jnp.concatenate(
                 [jnp.broadcast_to(v, (8, LANES)) for v in (lse_t, lse_s, weight, benefit)]
                 + [jnp.zeros((LANES - 32, LANES), f32)], axis=0)
-            ycol[b * LANES:(b + 1) * LANES, :] = y.T
-
-        @pl.loop(0, NG)
-        def _(i):
-            at = own_rows(far, i)
-            here = pl.ds(pl.multiple_of(i * PIECE, PIECE), PIECE)
-            lse_t, lse_s = ycol[here, 0:1], ycol[here, 8:9]
-            weight, benefit = ycol[here, 16:17], ycol[here, 24:25]
-            tp, sp = jnp.exp(part[1, at, :] - lse_t), jnp.exp(part[0, at, :] - lse_s)
-            hit = (column == acol[here, 0:1].astype(i32)).astype(f32)
-            g = weight * (KL_WEIGHT * (sp - tp) + benefit * (sp - hit))
-            grads[at, :] = g.astype(bf16)
-            for n in range(PIECE // GPIECE):
-                g_copy(upper, i * (PIECE // GPIECE) + n).start()
+            skip = c * CHUNK % LANES
+            ycol[c * CHUNK:(c + 1) * CHUNK, :] = y.T[skip:skip + CHUNK, :]
+
+            @pl.loop(first, last)
+            def _(i):
+                at = own_rows(far, i)
+                here = pl.ds(pl.multiple_of(i * PIECE, PIECE), PIECE)
+                lse_t, lse_s = ycol[here, 0:1], ycol[here, 8:9]
+                weight, benefit = ycol[here, 16:17], ycol[here, 24:25]
+                tp, sp = jnp.exp(part[1, at, :] - lse_t), jnp.exp(part[0, at, :] - lse_s)
+                hit = (column == acol[here, 0:1].astype(i32)).astype(f32)
+                g = weight * (KL_WEIGHT * (sp - tp) + benefit * (sp - hit))
+                grads[at, :] = g.astype(bf16)
+                for n in range(PIECE // GPIECE):
+                    g_copy(upper, i * (PIECE // GPIECE) + n).start()
+
+        for c in range(NC):
+            finish_chunk(c)
 
         for k in range(1, D // 2):
             loss_copy(k).start()
@@ -296,16 +313,20 @@
         def _(c):
             cols = pl.ds(pl.multiple_of(c * ftile, ftile), ftile)
             y = lax.dot_general(grads[at, :], ws[cols, :], (((1,), (1,)), ((), ())), preferred_element_type=f32)
-            hg[pl.ds(half * (J // 2), J // 2), :, :, cols] = y.reshape(J // 2, 2, TB, ftile)
+            part[0, at, cols] = y
+
+    def hg(b, c):
+        at = pl.ds(pl.multiple_of((b * 2 + c) * TB, TB), TB)
+        return part.at[0, at, :feature]
 
     def pair_copy(b):
-        return remote(hg.at[b, 1 - core], pair_in.at[b], hp_send.at[b], hp_recv.at[b], fsdp=partner)
+        return remote(hg(b, 1 - core), pair_in.at[b], hp_send.at[b], hp_recv.at[b], fsdp=partner)
 
     def hd_copy(b):
-        return remote(hg.at[b, core], peer_in.at[j], hd_send.at[b], hd_recv.at[j], fsdp=b * 2 + core)
+        return remote(hg(b, core), peer_in.at[j], hd_send.at[b], hd_recv.at[j], fsdp=b * 2 + core)
 
     def hd_in(b):
-        return remote(hg.at[b, core], peer_in.at[b], hd_send.at[b], hd_recv.at[b], fsdp=f)
+        return remote(hg(b, core), peer_in.at[b], hd_send.at[b], hd_recv.at[b], fsdp=f)
 
     def pair_start(half):
         @pl.loop(0, J // 2)
@@ -317,7 +338,7 @@
         def _(n):
             b = half * (J // 2) + n
             pair_copy(b).wait()
-            y = hg[b, core] + pair_in[b]
+            y = hg(b, core)[...] + pair_in[b]
 
             @pl.when(b == j)
             def _():
@@ -325,7 +346,7 @@
 
             @pl.when(b != j)
             def _():
-                hg[b, core] = y
+                hg(b, core)[...] = y
                 hd_copy(b).start()
 
     @pl.when(jnp.logical_not(end))
@@ -361,7 +382,8 @@
     @pl.when(jnp.logical_not(end))
     def _():
         loss_copy(0).wait_recv()
-    losses = jnp.concatenate([lossbuf[b * 8:b * 8 + 1, :] for b in range(nblk)], axis=1)
+    losses = jnp.concatenate(
+        [lossbuf[c * 8:c * 8 + 1, c * CHUNK % LANES:c * CHUNK % LANES + CHUNK] for c in range(NC)], axis=1)
     share = T // D
     for q in range(D // 2):
         @pl.when(lax.rem(r, D // 2) == q)
@@ -393,7 +415,8 @@
     @pl.when(end)
     def _():
         for k in range(1, F):
-            st_copy(k).wait_send()
+            for c in range(NC):
+                st_copy(c, k).wait_send()
         for k in range(1, D // 2):
             loss_copy(k).wait_send()
 
@@ -412,8 +435,7 @@
 
 
 def head_grad_kernel(rows_ref, grad_ref, out_ref):
-    out_ref[...] = lax.dot_general(
-        rows_ref[...], grad_ref[...], (((0,), (0,)), ((), ())), preferred_element_type=f32)
+    out_ref[...] = jnp.dot(rows_ref[...], grad_ref[...], preferred_element_type=f32)
 
 
 def shards(F, D, teacher_hidden, student_hidden, teacher_head, student_head, actions, advantages, loss_mask):
@@ -422,7 +444,7 @@
     ks = student_head.shape[0]
     mine = teacher_hidden.shape[0]
     J, H, TB = F // 2, T // 2, T // F
-    NG, GG, nblk = H // PIECE, H // GPIECE, H // LANES
+    NG, GG, NC = H // PIECE, H // GPIECE, H // CHUNK
     vmem = pl.BlockSpec(memory_space=pltpu.VMEM)
     hbm = pl.BlockSpec(memory_space=pl.ANY)
     dma = pltpu.SemaphoreType.DMA
@@ -431,7 +453,7 @@
         out_shape=(
             jax.ShapeDtypeStruct((1, T // D), f32),
             jax.ShapeDtypeStruct((TB, ks), bf16),
-            jax.ShapeDtypeStruct((T, ks), bf16),
+            jax.ShapeDtypeStruct((ks, T), bf16),
             jax.ShapeDtypeStruct((T, V), bf16),
         ),
         in_specs=[vmem, vmem, hbm, hbm, vmem, vmem, vmem],
@@ -448,12 +470,11 @@
             pltpu.VMEM((2, T, V), f32),
             pltpu.VMEM((2, 2 * NG, PIECE, V + LANES), i16),
             pltpu.VMEM((H, LANES), f32),
-            pltpu.VMEM((F, nblk * 8, LANES), f32),
+            pltpu.VMEM((NC, F, 8, LANES), f32),
             pltpu.VMEM((H, LANES), f32),
             pltpu.VMEM((H, LANES), f32),
-            pltpu.VMEM((nblk * 8, LANES), f32),
+            pltpu.VMEM((NC * 8, LANES), f32),
             pltpu.VMEM((T, V), bf16),
-            pltpu.VMEM((J, 2, TB, ks), f32),
             pltpu.VMEM((J, TB, ks), f32),
             pltpu.VMEM((J, TB, ks), f32),
             dma((2,)),
@@ -461,7 +482,7 @@
             dma((2, J)), dma((2, J)),
             dma((2, J)), dma((2, J)),
             dma((2, 2 * NG)), dma((2, 2 * NG)),
-            dma((F,)), dma((F,)),
+            dma((NC, F)), dma((NC, F)),
             dma((2, GG)), dma((2, GG)),
             dma((J,)), dma((J,)),
             dma((J,)), dma((J,)),
@@ -477,7 +498,7 @@
         head_grad_kernel,
         grid=(V // tile,),
         out_shape=jax.ShapeDtypeStruct((ks, V), f32),
-        in_specs=[pl.BlockSpec((T, ks), lambda c: (0, 0)), pl.BlockSpec((T, tile), lambda c: (0, c))],
+        in_specs=[pl.BlockSpec((ks, T), lambda c: (0, 0)), pl.BlockSpec((T, tile), lambda c: (0, c))],
         out_specs=pl.BlockSpec((ks, tile), lambda c: (0, c)),
         compiler_params=pltpu.CompilerParams(vmem_limit_bytes=63 * 2**20),
     )(rows, grads)

time: 103 us -> 96.7 us (0.939)
  Pallas kernels: 100 us -> 94.6 us
    pallas_call x1, Pallas kernels: 92.7 us -> 87.1 us  [shards(): pl.pallas_call(functools.partial(main_kernel, F, D), out_shape=(jax.Shape...]
where the time goes in v3:
time: 96.7 us; the launch traced here: 96.4 us
  Pallas kernels  94.6 us (98%)
  local copies, waits for them, and re-layouts  1.15 us (1%)
    pallas_call x1, Pallas kernels, shards(): pl.pallas_call(functools.partial(main_kernel, F, D), out_shape=(jax.Shape...  87.1 us
    pallas_call x1, Pallas kernels, shards(): pl.pallas_call(head_grad_kernel, grid=(V // tile,), out_shape=jax.ShapeDt...  7.48 us

profile of v3, /device:TPU:0, one launch (start us, length us, event | category | flops | bytes accessed | tf_op | source)
XLA Modules:
  0.0 96.4 jit_solution(6589045544600545502)
XLA Ops:
  0.6 87.1 %shard_map.94 = (f32[1,64]{1,0:T(1,128)}, bf16[32,1024]{1,0:T(8,128)(2,1)}, bf16[1024,256]{1,0:T(8,128)(2,1)}, bf16[256,2048]{1,0:T(8,128)(2,1)}) custom-call(bf16[8,8192]{1,0:T(8,128)(2,1)} %th_ref.1, bf16[8,4096]{1,0:T(8,128)(2,1)} %sh_ref.1, bf16[2048,2048]{1,0:T(8,128)(2,1)} %wt_hbm.1, bf16[1024,2048]{1,0:T(8,128)(2,1)} %ws_hbm.1, s32[1,256]{1,0:T(1,128)} %bitcast.4, ...), custom_call_target="tpu_custom_call" | custom-call | tf_op jit(solution)/shard_map/pallas_call | solution.py:451
  87.8 0.0 copy-start.1
  87.8 0.0 copy-start
  87.8 7.5 %shard_map.95 = f32[1024,2048]{1,0:T(8,128)} custom-call(bf16[1024,256]{1,0:T(8,128)(2,1)} %get-tuple-element.8.rows_ref, bf16[256,2048]{1,0:T(8,128)(2,1)} %get-tuple-element.9.grad_ref), custom_call_target="tpu_custom_call" | custom-call | tf_op jit(solution)/shard_map/pallas_call | solution.py:497
  95.3 0.0 copy-done.1
  95.3 0.5 copy.12
  95.8 0.0 copy-done
  95.8 0.6 copy.13
Async XLA Ops:
  87.8 7.5 %copy-start.1 = (f32[1,64]{1,0:T(1,128)S(1)}, f32[1,64]{1,0:T(1,128)}, u32[]{:S(2)}) copy-start(f32[1,64]{1,0:T(1,128)} %get-tuple-element.7) | copy-start | bytes 772
  87.8 8.0 %copy-start = (bf16[32,1024]{1,0:T(8,128)(2,1)S(1)}, bf16[32,1024]{1,0:T(8,128)(2,1)}, u32[]{:S(2)}) copy-start(bf16[32,1024]{1,0:T(8,128)(2,1)} %get-tuple-element.16) | copy-start | bytes 196612

commit v4 on v3

--- a/solution.py
+++ b/solution.py
@@ -9,14 +9,15 @@
 
 KL_WEIGHT = 0.5
 MESH = pl.DeviceIdType.MESH
-PIECE = 32
+PIECE = 16
 GPIECE = 16
-LAG = 2
+LAG = 4
 GLAG = 3
 CHUNK = 64
 LANES = 128
 STEPS = 128.0
 FULL = 32000.0
+MIDDLE = 32768
 f32, bf16, i32, i16 = jnp.float32, jnp.bfloat16, jnp.int32, jnp.int16
 
 
@@ -24,8 +25,8 @@
     cols = x.shape[1]
     top = jnp.maximum(jnp.max(jnp.abs(x), axis=1, keepdims=True), 1e-30)
     code = jnp.floor(jnp.log2(top) * STEPS) + 2.0
-    q = jnp.floor(x * (jnp.exp2(code * (-1.0 / STEPS)) * FULL) + 0.5)
-    out_ref[:, :cols] = q.astype(i32).astype(i16)
+    q = x * (jnp.exp2(code * (-1.0 / STEPS)) * FULL) + (MIDDLE + 0.5)
+    out_ref[:, :cols] = (q.astype(i32) - MIDDLE).astype(i16)
     out_ref[:, cols:] = jnp.broadcast_to(code, (x.shape[0], LANES)).astype(i32).astype(i16)
 
 
@@ -140,7 +141,7 @@
             rows[at, :half] = x[:, 0:8, :].reshape(n, half).astype(bf16)
             rows[at, half:] = x[:, 8:16, :].reshape(n, half).astype(bf16)
 
-    tile = max(LANES, min(V, 2**17 // T))
+    tile = max(LANES, min(V, 2**18 // T))
 
     def project(rows, w, m):
         @pl.loop(0, V // tile)
@@ -304,7 +305,7 @@
             loss_copy(k).start()
 
     feature = ws.shape[0]
-    ftile = min(256, feature)
+    ftile = min(512, feature)
 
     def back(half):
         at = pl.ds(pl.multiple_of(half * H, H), H)
@@ -493,13 +494,13 @@
             collective_id=0, has_side_effects=True, vmem_limit_bytes=63 * 2**20),
     )(teacher_hidden, student_hidden, teacher_head, student_head,
       actions.reshape(1, T), advantages.reshape(1, T), loss_mask.reshape(1, T))
-    tile = min(256, V)
+    tile = min(256, ks)
     head_grad = pl.pallas_call(
         head_grad_kernel,
-        grid=(V // tile,),
+        grid=(ks // tile,),
         out_shape=jax.ShapeDtypeStruct((ks, V), f32),
-        in_specs=[pl.BlockSpec((ks, T), lambda c: (0, 0)), pl.BlockSpec((T, tile), lambda c: (0, c))],
-        out_specs=pl.BlockSpec((ks, tile), lambda c: (0, c)),
+        in_specs=[pl.BlockSpec((tile, T), lambda c: (c, 0)), pl.BlockSpec((T, V), lambda c: (0, 0))],
+        out_specs=pl.BlockSpec((tile, V), lambda c: (c, 0)),
         compiler_params=pltpu.CompilerParams(vmem_limit_bytes=63 * 2**20),
     )(rows, grads)
     return loss.reshape(T // D), head_grad, hidden_grad

time: 96.7 us -> 94 us (0.972)
  Pallas kernels: 94.6 us -> 92 us
    pallas_call x1, Pallas kernels: 7.48 us -> 5.92 us  [shards(): pl.pallas_call(head_grad_kernel, grid=(ks // tile,), out_shape=jax.ShapeD...]
    pallas_call x1, Pallas kernels: 87.1 us -> 86.1 us  [shards(): pl.pallas_call(functools.partial(main_kernel, F, D), out_shape=(jax.Shape...]
where the time goes in v4:
time: 94 us; the launch traced here: 93.8 us
  Pallas kernels  92 us (98%)
  local copies, waits for them, and re-layouts  1.15 us (1%)
    pallas_call x1, Pallas kernels, shards(): pl.pallas_call(functools.partial(main_kernel, F, D), out_shape=(jax.Shape...  86.1 us
    pallas_call x1, Pallas kernels, shards(): pl.pallas_call(head_grad_kernel, grid=(ks // tile,), out_shape=jax.ShapeD...  5.92 us

profile of v4, /device:TPU:0, one launch (start us, length us, event | category | flops | bytes accessed | tf_op | source)
XLA Modules:
  0.0 93.8 jit_solution(16971595243814688912)
XLA Ops:
  0.6 86.1 %shard_map.94 = (f32[1,64]{1,0:T(1,128)}, bf16[32,1024]{1,0:T(8,128)(2,1)}, bf16[1024,256]{1,0:T(8,128)(2,1)}, bf16[256,2048]{1,0:T(8,128)(2,1)}) custom-call(bf16[8,8192]{1,0:T(8,128)(2,1)} %th_ref.1, bf16[8,4096]{1,0:T(8,128)(2,1)} %sh_ref.1, bf16[2048,2048]{1,0:T(8,128)(2,1)} %wt_hbm.1, bf16[1024,2048]{1,0:T(8,128)(2,1)} %ws_hbm.1, s32[1,256]{1,0:T(1,128)} %bitcast.4, ...), custom_call_target="tpu_custom_call" | custom-call | tf_op jit(solution)/shard_map/pallas_call | solution.py:452
  86.7 0.0 copy-start.1
  86.7 0.0 copy-start
  86.7 5.9 %shard_map.95 = f32[1024,2048]{1,0:T(8,128)} custom-call(bf16[1024,256]{1,0:T(8,128)(2,1)} %get-tuple-element.8.rows_ref, bf16[256,2048]{1,0:T(8,128)(2,1)} %get-tuple-element.9.grad_ref), custom_call_target="tpu_custom_call" | custom-call | tf_op jit(solution)/shard_map/pallas_call | solution.py:498
  92.7 0.0 copy-done.1
  92.7 0.5 copy.12
  93.2 0.0 copy-done
  93.2 0.6 copy.13
Async XLA Ops:
  86.7 5.9 %copy-start.1 = (f32[1,64]{1,0:T(1,128)S(1)}, f32[1,64]{1,0:T(1,128)}, u32[]{:S(2)}) copy-start(f32[1,64]{1,0:T(1,128)} %get-tuple-element.7) | copy-start | bytes 772
  86.7 6.5 %copy-start = (bf16[32,1024]{1,0:T(8,128)(2,1)S(1)}, bf16[32,1024]{1,0:T(8,128)(2,1)}, u32[]{:S(2)}) copy-start(bf16[32,1024]{1,0:T(8,128)(2,1)} %get-tuple-element.16) | copy-start | bytes 196612
